TPU v7x, 32 devices: a whole 2x2x4 slice. The times are simulated.
32 devices in a mesh: space: 8 (over y, x, core), vel: 4 (over z).
Axes of the slice: x: 2, y: 2, z: 4, core: 2. Of those that a mesh axis runs over, the one named last changes fastest.
Arguments:
- distribution: float32 [4096, 8192], P('vel', 'space'), may hold values from -48 to 48
- kernel: bfloat16 [4096, 4096], P('vel'), may hold values from -0.046875 to 0.046875
- frequency: float32 [4096], P('vel'), may hold values from 0.05 to 0.5
- accommodation: float32 [8], replicated, may hold values from 0.2 to 0.95
- wall_class: int32 [2, 256], P(None, 'space'), may hold values from 0 to 7
Outputs:
- updated: float32 [4096, 8192], P('vel', 'space')
All inputs are finite; a program needn't handle non-finite values.
Results may differ from a plain program's by a relative error of at most 0.0018.
Values may be sent and summed in bfloat16 or wider, within the bound.
A program may use at most 128 MiB of HBM per device.

v0:
```python
import jax
import jax.numpy as jnp
from jax import lax
from jax.sharding import PartitionSpec as P

NV1 = 16
NY = 32
NCLASS = 8


courant_x = 0.05
courant_y = 0.15


def swapped(value, axis, distance):
    return lax.ppermute(value, axis, [(i, i ^ 1 << distance) for i in range(lax.axis_size(axis))])


def extended(value, sides, width):
    for axis, dim in sides:
        devices, length = (lax.axis_size(axis), value.shape[dim])
        up = [(i, (i + 1) % devices) for i in range(devices)]
        down = [(j, i) for i, j in up]
        last = lax.slice_in_dim(value, length - width, length, axis=dim)
        initial = lax.slice_in_dim(value, 0, width, axis=dim)
        before = lax.ppermute(last, axis, up)
        after = lax.ppermute(initial, axis, down)
        value = jnp.concatenate([before, value, after], axis=dim)
    return value


def velocity_parts(vel_index):
    spacing = 9.6 / NV1
    middle = (NV1 - 1) / 2.0
    index_y = vel_index // (NV1 * NV1)
    index_x = vel_index // NV1 % NV1
    index_z = vel_index % NV1
    vel_x = (index_x.astype(jnp.float32) - middle) * spacing
    vel_y = (index_y.astype(jnp.float32) - middle) * spacing
    vel_z = (index_z.astype(jnp.float32) - middle) * spacing
    return (vel_x, vel_y, vel_z)


def grid_constants():
    spacing = 9.6 / NV1
    middle = (NV1 - 1) / 2.0
    points = (lax.iota(jnp.int32, NV1).astype(jnp.float32) - middle) * spacing
    weights = jnp.exp(-0.5 * points * points)
    zsum = jnp.sum(weights)
    outflow = jnp.sum(jnp.where(points > 0, points * weights, 0.0)) / zsum
    return (zsum * zsum * zsum, outflow)


def per_device(distribution, kernel, frequency, accommodation, wall_class):
    vel_rows, cell_count = distribution.shape
    columns = cell_count // NY
    plane = NV1 * NV1
    rank = lax.axis_index("vel")
    vel_index = rank * vel_rows + lax.iota(jnp.int32, vel_rows)
    vel_x, vel_y, vel_z = velocity_parts(vel_index)
    normal_sum, outflow = grid_constants()
    maxwell = jnp.exp(-0.5 * (vel_x * vel_x + vel_y * vel_y + vel_z * vel_z)) / normal_sum
    lowered = distribution.astype(jnp.bfloat16)
    walls = jnp.stack([lowered[:, 0::NY], lowered[:, NY - 1 :: NY]])
    wide = walls.astype(jnp.float32)
    down_weight = jnp.where(vel_y < 0, -vel_y, 0.0)
    up_weight = jnp.where(vel_y > 0, vel_y, 0.0)
    partial_flux = jnp.stack(
        [
            jnp.sum(down_weight[:, None] * wide[0], axis=0),
            jnp.sum(up_weight[:, None] * wide[1], axis=0),
        ]
    )
    flux = lax.psum(partial_flux, "vel")
    mirrored = walls
    log_rows = vel_rows.bit_length() - 1
    log_devices = lax.axis_size("vel").bit_length() - 1
    log_plane = 2 * (NV1.bit_length() - 1)
    for bit_index in range(max(log_plane - log_rows, 0), log_devices):
        mirrored = swapped(mirrored, "vel", bit_index)
    if vel_rows > plane:
        mirrored = mirrored.reshape(2, vel_rows // plane, plane, columns)[:, ::-1].reshape(
            2, vel_rows, columns
        )
    mirrored = mirrored.astype(jnp.float32)
    sigma = flux / outflow
    class_ids = lax.iota(jnp.int32, NCLASS)
    alpha = jnp.sum(
        jnp.where(
            wall_class[:, :, None] == class_ids[None, None, :], accommodation[None, None, :], 0.0
        ),
        axis=2,
    )
    inflow = (
        alpha[:, None, :] * sigma[:, None, :] * maxwell[None, :, None]
        + (1.0 - alpha)[:, None, :] * mirrored
    )
    padded = extended(distribution.astype(jnp.bfloat16), (("space", 1),), NY).astype(
        distribution.dtype
    )
    left = padded[:, :cell_count]
    right = padded[:, 2 * NY :]
    y_place = lax.iota(jnp.int32, cell_count) % NY
    below = jnp.concatenate([distribution[:, :1], distribution[:, :-1]], axis=1)
    below = jnp.where(y_place[None, :] == 0, jnp.repeat(inflow[0], NY, axis=1), below)
    above = jnp.concatenate([distribution[:, 1:], distribution[:, -1:]], axis=1)
    above = jnp.where(y_place[None, :] == NY - 1, jnp.repeat(inflow[1], NY, axis=1), above)
    move_x = courant_x * (
        jnp.maximum(vel_x, 0.0)[:, None] * (distribution - left)
        + jnp.minimum(vel_x, 0.0)[:, None] * (right - distribution)
    )
    move_y = courant_y * (
        jnp.maximum(vel_y, 0.0)[:, None] * (distribution - below)
        + jnp.minimum(vel_y, 0.0)[:, None] * (above - distribution)
    )
    moved = move_x + move_y
    shard_piece = lax.all_gather(lowered, "vel", axis=0, tiled=True)
    running = jnp.dot(kernel, shard_piece, preferred_element_type=jnp.float32)
    piece_walls = jnp.stack([shard_piece[:, 0::NY], shard_piece[:, NY - 1 :: NY]])
    wall_store = piece_walls
    gain, wall_store = (running, wall_store)
    return distribution - moved - frequency[:, None] * distribution + gain


def solution(mesh):
    placed = (P("vel", "space"), P("vel", None), P("vel"), P(), P(None, "space"))
    return jax.shard_map(
        per_device, mesh=mesh, in_specs=placed, out_specs=P("vel", "space"), check_vma=False
    )
```

profile of v0, /device:TPU:0, one launch (start us, length us, event | category | flops | bytes accessed | tf_op | source)
XLA Modules:
  0.0 196.7 jit_solution(3990683723078909586)
XLA Ops:
  6.5 0.0 all-gather.2.cloned.1.call-start
  6.5 3.8 %convert_element_type.63 = bf16[1024,1024]{1,0:T(8,128)(2,1)} convert(f32[1024,1024]{1,0:T(8,128)} %param.5) | non-fusion elementwise | flops 1048576 | bytes 6291456 | tf_op jit(solution)/shard_map/convert_element_type | solution.py:98
  10.4 0.0 all-gather.2.cloned.1.call-update
  10.4 5.0 %slice.47 = bf16[1024,32]{1,0:T(8,128)(2,1)S(1)} slice(bf16[1024,1024]{1,0:T(8,128)(2,1)} %convert_element_type.63), slice={[0:1024:1], [31:1024:32]} | slice | bytes 131072 | tf_op jit(solution)/shard_map/slice | solution.py:64
  15.4 4.8 %slice.46 = bf16[1024,32]{1,0:T(8,128)(2,1)S(1)} slice(bf16[1024,1024]{1,0:T(8,128)(2,1)} %convert_element_type.63), slice={[0:1024:1], [0:1024:32]} | slice | bytes 131072 | tf_op jit(solution)/shard_map/slice | solution.py:64
  20.2 0.1 copy.14
  20.4 0.1 copy.13
  20.5 3.1 %collective-permute-start.2 = (bf16[2,1024,32]{1,2,0:T(8,128)(2,1)S(1)}, bf16[2,1024,32]{1,2,0:T(8,128)(2,1)}, u32[]{:S(2)}, u32[]{:S(2)}) collective-permute-start(bf16[2,1024,32]{1,2,0:T(8,128)(2,1)S(1)} %get-tuple-element.16), channel_id=1, source_target_pairs={{0,1},{1,0},{2,3},{3,2},{4,5},{5,4},{6,7},{7,6},{8,9},{9,8},{10,11... | collective-permute-start | bytes 393224 | tf_op jit(solution)/shard_map/ppermute | solution.py:16
  23.6 0.0 copy-done
  23.6 1.0 fusion.50
  24.6 1.6 collective-permute-start.1
  26.2 0.0 collective-permute-start
  26.2 0.6 fusion.46
  26.8 0.6 fusion.44
  28.5 0.1 fusion.17
  28.7 15.5 %psum.7 = f32[2,32]{1,0:T(2,128)S(1)} all-reduce(f32[2,32]{1,0:T(2,128)S(1)} %pad_maximum_fusion.1), channel_id=1, replica_groups=mesh['space'=8,'vel'=4] {'vel'}, use_global_device_ids=true, to_apply=%region_3.4 | all-reduce | flops 64 | bytes 512 | tf_op jit(solution)/shard_map/psum | solution.py:74
  44.2 0.0 copy-done.4
  44.2 0.0 copy-done.7
  44.2 0.1 select_reduce_fusion
  44.3 1.4 fusion.49
  45.7 8.1 %fusion.48 = (f32[1024,1023]{1,0:T(8,128)}, f32[1024,1023]{1,0:T(8,128)}) fusion(f32[1024,1024]{1,0:T(8,128)} %param.5), kind=kLoop, calls=%fused_computation.87 | loop fusion | bytes 16760832 | tf_op jit(solution)/shard_map/slice | solution.py:106
  53.9 0.6 broadcast_minimum_fusion.1
  56.1 0.6 broadcast_minimum_fusion
  56.7 0.0 collective-permute-done.2
  56.7 0.0 collective-permute-start.3
  56.7 0.6 fusion.36
  57.3 0.0 collective-permute-done.1
  57.3 0.0 collective-permute-done
  57.3 4.5 %concatenate.9 = bf16[1024,1088]{1,0:T(8,128)(2,1)} concatenate(bf16[1024,32]{1,0:T(8,128)(2,1)} %collective-permute-done, bf16[1024,1024]{1,0:T(8,128)(2,1)S(1)} %copy-done, bf16[1024,32]{1,0:T(8,128)(2,1)S(1)} %collective-permute-done.1), dimensions={1} | concatenate | bytes 4456448 | tf_op jit(solution)/shard_map/concatenate | solution.py:28
  61.9 4.1 %convert_element_type.64 = f32[1024,1088]{1,0:T(8,128)} convert(bf16[1024,1088]{1,0:T(8,128)(2,1)} %concatenate.9) | non-fusion elementwise | flops 1114112 | bytes 6684672 | tf_op jit(solution)/shard_map/convert_element_type | solution.py:98
  66.0 6.7 %collective-permute-done.3 = bf16[2,1024,32]{1,2,0:T(8,128)(2,1)S(1)} collective-permute-done((bf16[2,1024,32]{1,2,0:T(8,128)(2,1)}, bf16[2,1024,32]{1,2,0:T(8,128)(2,1)S(1)}, u32[]{:S(2)}, u32[]{:S(2)}) %collective-permute-start.3) | collective-permute-done | bytes 131104 | tf_op jit(solution)/shard_map/ppermute | solution.py:16
  72.8 0.1 reshape.168
  72.8 0.3 rev.3
  73.2 0.1 reshape.171
  73.2 0.1 multiply_add_fusion
  73.4 2.5 %broadcast_in_dim.57 = f32[1024,32,32]{0,2,1:T(8,128)} broadcast(f32[1024,32]{0,1:T(8,128)S(1)} %get-tuple-element.13), dimensions={0,1} | broadcast | bytes 4325376 | tf_op jit(solution)/shard_map/broadcast_in_dim | solution.py:107
  75.9 5.4 %copy.16 = f32[1024,1024]{1,0:T(8,128)} copy(f32[1024,1024]{0,1:T(8,128)} %bitcast.28) | data formatting | bytes 8388608 | tf_op jit(solution)/shard_map/reshape | solution.py:107
  81.3 2.5 %broadcast_in_dim.55 = f32[1024,32,32]{0,2,1:T(8,128)} broadcast(f32[1024,32]{0,1:T(8,128)S(1)} %get-tuple-element.14), dimensions={0,1} | broadcast | bytes 4325376 | tf_op jit(solution)/shard_map/broadcast_in_dim | solution.py:105
  83.9 0.0 copy-start.6
  83.9 0.0 copy-start.8
  83.9 5.5 %copy.15 = f32[1024,1024]{1,0:T(8,128)} copy(f32[1024,1024]{0,1:T(8,128)} %bitcast.29) | data formatting | bytes 8388608 | tf_op jit(solution)/shard_map/reshape | solution.py:105
  89.4 79.4 %all-gather.2.cloned.1.call-done = bf16[4096,1024]{1,0:T(8,128)(2,1)} async-done(((bf16[1024,1024]{1,0:T(8,128)(2,1)}), bf16[4096,1024]{1,0:T(8,128)(2,1)}) %all-gather.2.cloned.1.call-update) | async-done | bytes 8388624 | tf_op jit(solution)/shard_map/all_gather | solution.py:117
  168.8 0.0 copy-done.1
  168.8 0.0 copy-done.2
  168.8 0.0 copy-done.3
  168.8 0.0 copy-done.5
  168.8 0.0 copy-done.6
  168.8 21.0 %fusion.6 = f32[1024,1024]{1,0:T(8,128)} fusion(f32[1024,1024]{1,0:T(8,128)} %param.5, f32[1024,1088]{1,0:T(8,128)} %convert_element_type.64, f32[1024,1024]{1,0:T(8,128)} %copy.15, f32[1024,1023]{1,0:T(8,128)} %get-tuple-element.8, f32[1024,1]{1,0:T(8,128)S(1)} %get-tuple-element.10, f32[1024,1024]{1,0:T(8,128)} %copy.16, ...), kind=kOutput, calls=%fused_computation.7 | convolution fusion | flops 8611954688 | bytes 50354176 | tf_op jit(solution)/shard_map/dot_general | solution.py:118
  (14 shorter events, 0.1 us)
Async XLA Ops:
  6.5 162.3 %all-gather.2.cloned.1.call-start = ((), (), s32[]{:S(2)}) async-start(), calls=%async_computation | async-start | bytes 10485760 | tf_op jit(solution)/shard_map/all_gather | solution.py:117
  10.4 13.3 %copy-start = (bf16[1024,1024]{1,0:T(8,128)(2,1)S(1)}, bf16[1024,1024]{1,0:T(8,128)(2,1)}, u32[]{:S(2)}) copy-start(bf16[1024,1024]{1,0:T(8,128)(2,1)} %convert_element_type.63) | copy-start | bytes 6291460
  10.4 33.9 %copy-start.4 = (s32[2,32]{1,0:T(2,128)S(1)}, s32[2,32]{1,0:T(2,128)}, u32[]{:S(2)}) copy-start(s32[2,32]{1,0:T(2,128)} %param.9) | copy-start | bytes 772
  10.4 33.9 %copy-start.7 = (f32[8]{0:T(128)S(1)}, f32[8]{0:T(128)}, u32[]{:S(2)}) copy-start(f32[8]{0:T(128)} %param.8) | copy-start | bytes 100
  20.5 36.2 %collective-permute-start.2 = (bf16[2,1024,32]{1,2,0:T(8,128)(2,1)S(1)}, bf16[2,1024,32]{1,2,0:T(8,128)(2,1)}, u32[]{:S(2)}, u32[]{:S(2)}) collective-permute-start(bf16[2,1024,32]{1,2,0:T(8,128)(2,1)S(1)} %get-tuple-element.16), channel_id=1, source_target_pairs={{0,1},{1,0},{2,3},{3,2},{4,5},{5,4},{6,7},{7,6},{8,9},{9,8},{10,11... | collective-permute-start | bytes 393224 | tf_op jit(solution)/shard_map/ppermute | solution.py:16
  24.6 32.8 %collective-permute-start.1 = (bf16[1024,32]{1,0:T(8,128)(2,1)}, bf16[1024,32]{1,0:T(8,128)(2,1)S(1)}, u32[]{:S(2)}, u32[]{:S(2)}) collective-permute-start(bf16[1024,32]{1,0:T(8,128)(2,1)} %get-tuple-element.11), channel_id=1, source_target_pairs={{4,0},{8,4},{12,8},{16,12},{20,16},{24,20},{28,24},{0,28},{5,1},{9... | collective-permute-start | bytes 196616 | tf_op jit(solution)/shard_map/ppermute | solution.py:27
  26.2 31.2 %collective-permute-start = (bf16[1024,32]{1,0:T(8,128)(2,1)}, bf16[1024,32]{1,0:T(8,128)(2,1)}, u32[]{:S(2)}, u32[]{:S(2)}) collective-permute-start(bf16[1024,32]{1,0:T(8,128)(2,1)} %get-tuple-element.12), channel_id=1, source_target_pairs={{0,4},{4,8},{8,12},{12,16},{16,20},{20,24},{24,28},{28,0},{1,5},{5... | collective-permute-start | bytes 196616 | tf_op jit(solution)/shard_map/ppermute | solution.py:26
  56.7 16.0 %collective-permute-start.3 = (bf16[2,1024,32]{1,2,0:T(8,128)(2,1)}, bf16[2,1024,32]{1,2,0:T(8,128)(2,1)S(1)}, u32[]{:S(2)}, u32[]{:S(2)}) collective-permute-start(bf16[2,1024,32]{1,2,0:T(8,128)(2,1)} %collective-permute-done.2), channel_id=1, source_target_pairs={{0,2},{1,3},{2,0},{3,1},{4,6},{5,7},{6,4},{7,5},{8,10},{9,11},{10,... | collective-permute-start | bytes 393224 | tf_op jit(solution)/shard_map/ppermute | solution.py:16
  83.9 85.0 %copy-start.1 = (f32[1024]{0:T(1024)S(1)}, f32[1024]{0:T(1024)}, u32[]{:S(2)}) copy-start(f32[1024]{0:T(1024)} %get-tuple-element.24) | copy-start | bytes 12292
  83.9 85.0 %copy-start.2 = (f32[1024]{0:T(1024)S(1)}, f32[1024]{0:T(1024)}, u32[]{:S(2)}) copy-start(f32[1024]{0:T(1024)} %get-tuple-element.21) | copy-start | bytes 12292
  83.9 85.0 %copy-start.3 = (f32[1024]{0:T(1024)S(1)}, f32[1024]{0:T(1024)}, u32[]{:S(2)}) copy-start(f32[1024]{0:T(1024)} %get-tuple-element.22) | copy-start | bytes 12292
  83.9 85.0 %copy-start.5 = (pred[1024]{0:T(1024)(128)(4,1)S(1)}, pred[1024]{0:T(1024)(128)(4,1)}, u32[]{:S(2)}) copy-start(pred[1024]{0:T(1024)(128)(4,1)} %get-tuple-element.25) | copy-start | bytes 3076
  83.9 85.0 %copy-start.6 = (pred[1024]{0:T(1024)(128)(4,1)S(1)}, pred[1024]{0:T(1024)(128)(4,1)}, u32[]{:S(2)}) copy-start(pred[1024]{0:T(1024)(128)(4,1)} %get-tuple-element.26) | copy-start | bytes 3076
  83.9 85.0 %copy-start.8 = (f32[1024]{0:T(1024)S(1)}, f32[1024]{0:T(1024)}, u32[]{:S(2)}) copy-start(f32[1024]{0:T(1024)} %param.7) | copy-start | bytes 12292
Sparse Core Ops, SparseCore 0:
  10.5 158.2 all-gather.1
where the time goes:
time: 197 us
  waiting for transfers between devices  86.2 us (44%)
  local copies, waits for them, and re-layouts  41.6 us (21%)
  matrix products  21 us (11%)
  between operations  16.3 us (8%)
  blocking collectives  15.5 us (8%)
  other arithmetic  11.4 us (6%)
  starting transfers between devices  4.71 us (2%)
    all_gather x1, waiting for transfers between devices, per_device(): shard_piece = lax.all_gather(lowered, 'vel', axis=0, tiled=True)  79.4 us
    dot_general x1, matrix products, per_device(): running = jnp.dot(kernel, shard_piece, preferred_element_type=jnp.float32)  21 us
    psum x1, blocking collectives, per_device(): flux = lax.psum(partial_flux, 'vel')  15.5 us
    slice x2, local copies, waits for them, and re-layouts, per_device(): walls = jnp.stack([lowered[:, 0::NY], lowered[:, NY - 1::NY]])  9.83 us
    slice x2, local copies, waits for them, and re-layouts, per_device(): above = jnp.concatenate([distribution[:, 1:], distribution[:, -1:]], axis=1)  9.52 us
    ppermute x2, waiting for transfers between devices, swapped(): lax.ppermute(value, axis, [(i, i ^ 1 << distance) for i in range(lax.axis...  6.73 us
    reshape x1, local copies, waits for them, and re-layouts, per_device(): jnp.repeat(inflow[0], NY, axis=1)  5.52 us
    reshape x1, local copies, waits for them, and re-layouts, per_device(): jnp.repeat(inflow[1], NY, axis=1)  5.39 us
  transfers between devices with their start and end apart: 5, of which 2 were waited for; matrix products, arithmetic and copies ran while one was open for 25% of the time, Pallas kernels for 0%

commit v1 on v0

--- a/solution.py
+++ b/solution.py
@@ -1,6 +1,8 @@
 import jax
 import jax.numpy as jnp
 from jax import lax
+from jax.experimental import pallas as pl
+from jax.experimental.pallas import tpu as pltpu
 from jax.sharding import PartitionSpec as P
 
 NV1 = 16
@@ -122,8 +124,322 @@
     return distribution - moved - frequency[:, None] * distribution + gain
 
 
+WIDE = 128
+ROWS = 1024
+TILE = NV1 * NV1
+PARTS = 4
+SPACE = 8
+
+
+def gain_kernel(dist, kern, coef, lanes, out, d32, ks, ke, db, pb, hl,
+                lsem, s1, r1, s2, r2, s3, r3, s4, r4, sk, rk, sh, rh):
+    chunks = dist.shape[1] // WIDE
+    sp, z = lax.axis_index("space"), lax.axis_index("vel")
+    half = lax.div(z, 2)
+    mid = lax.rem(z, 2) + half == 1
+    mate = z + 1 - 2 * lax.rem(z, 2)
+    peer = 3 - z
+    far = 3 - mate
+    by_core = sp + 1 - 2 * lax.rem(sp, 2)
+    by_x = sp + 2 - 4 * lax.rem(lax.div(sp, 2), 2)
+    by_y = sp + 4 - 8 * lax.div(sp, 4)
+    by_xy = by_x + by_y - sp
+    right = lax.rem(sp + 1, SPACE)
+    left = lax.rem(sp + SPACE - 1, SPACE)
+
+    def remote(src, dst, send, recv, space, vel):
+        return pltpu.make_async_remote_copy(
+            src_ref=src, dst_ref=dst, send_sem=send, recv_sem=recv,
+            device_id={"space": space, "vel": vel}, device_id_type=pl.DeviceIdType.MESH)
+
+    load_d = pltpu.make_async_copy(dist, d32, lsem.at[0])
+    load_k = pltpu.make_async_copy(kern, ks, lsem.at[1])
+    load_d.start()
+    load_k.start()
+
+    barrier = pltpu.get_barrier_semaphore()
+
+    def greet(space, vel):
+        pl.semaphore_signal(barrier, inc=1, device_id={"space": space, "vel": vel},
+                            device_id_type=pl.DeviceIdType.MESH)
+
+    greet(sp, mate)
+    greet(left, z)
+    greet(right, z)
+
+    @pl.when(mid)
+    def _():
+        greet(sp, peer)
+        greet(by_core, z)
+        greet(by_x, z)
+        greet(by_y, z)
+        pl.semaphore_wait(barrier, 7)
+
+    @pl.when(jnp.logical_not(mid))
+    def _():
+        pl.semaphore_wait(barrier, 3)
+
+    def slab(owner):
+        return ke.at[pl.ds(pl.multiple_of(owner * (ROWS // SPACE), ROWS // SPACE), ROWS // SPACE)]
+
+    slab_rows = pl.ds(pl.multiple_of(sp * (ROWS // SPACE), ROWS // SPACE), ROWS // SPACE)
+    slab_cols = pl.ds(pl.multiple_of((1 - half) * 2 * ROWS, 2 * ROWS), 2 * ROWS)
+    kern_out = remote(kern.at[slab_rows, slab_cols], slab(sp), sk.at[0], rk.at[0], sp, mate)
+
+    to_mate = lambda c: remote(db.at[0, c], db.at[1, c], s1.at[c], r1.at[c], sp, mate)
+    to_peer = lambda c: remote(db.at[0, c], db.at[2, c], s2.at[c], r2.at[c], sp, peer)
+    pass_on = lambda c: remote(db.at[1, c], db.at[3, c], s3.at[c], r3.at[c], sp, peer)
+    partial = lambda c: remote(pb.at[c], pb.at[c], s4.at[c], r4.at[c], sp, mate)
+    to_right = remote(db.at[0, chunks - 1], hl.at[0], sh.at[0], rh.at[0], right, z)
+    to_left = remote(db.at[0, 0], hl.at[1], sh.at[1], rh.at[1], left, z)
+
+    def plan(out_slab, in_slab, at, target):
+        return (remote(slab(out_slab), slab(out_slab), sk.at[at], rk.at[at], target, z),
+                remote(slab(in_slab), slab(in_slab), sk.at[at], rk.at[at], target, z))
+
+    over_x = plan(sp, by_x, 1, by_x)
+    over_y = plan(sp, by_y, 2, by_y)
+    over_xy = plan(by_x, by_xy, 3, by_y)
+    over_core = [plan(mine, mine + by_core - sp, 4 + i, by_core)
+                 for i, mine in enumerate((sp, by_x, by_y, by_xy))]
+
+    @pl.when(jnp.logical_not(mid))
+    def _():
+        kern_out.start()
+
+    load_d.wait()
+
+    def cols(c):
+        return pl.ds(pl.multiple_of(c * WIDE, WIDE), WIDE)
+
+    def rows(r):
+        return pl.ds(pl.multiple_of(r * TILE, TILE), TILE)
+
+    def loop(n, body):
+        def step(i, carry):
+            body(i)
+            return carry
+        lax.fori_loop(0, n, step, 0)
+
+    def span(lo, hi, body):
+        def step(i, carry):
+            body(i)
+            return carry
+        lax.fori_loop(lo, hi, step, 0)
+
+    def lower(c):
+        def tile(r):
+            db[0, c, rows(r), :] = d32[rows(r), cols(c)].astype(jnp.bfloat16)
+        loop(PARTS, tile)
+
+    def lower_send(c):
+        lower(c)
+
+        @pl.when(mid)
+        def _():
+            to_peer(c).start()
+            to_mate(c).start()
+
+    loop(chunks, lower_send)
+    to_right.start()
+    to_left.start()
+
+    @pl.when(jnp.logical_not(mid))
+    def _():
+        kern_out.wait_send()
+        loop(chunks, lambda c: to_mate(c).start())
+
+    load_k.wait()
+    to_right.wait_recv()
+    to_left.wait_recv()
+
+    lane = lax.broadcasted_iota(jnp.int32, (TILE, WIDE), 1)
+    low_wall = lax.rem(lane, NY) == 0
+    up_wall = lax.rem(lane, NY) == NY - 1
+
+    def dot(ref, r, block, slot, c):
+        k_cols = pl.ds(pl.multiple_of(block * ROWS, ROWS), ROWS)
+        return jnp.dot(ref[rows(r), k_cols], db[slot, c], preferred_element_type=jnp.float32)
+
+    def local(c):
+        prev_at = cols(jnp.maximum(c - 1, 0))
+        next_at = cols(jnp.minimum(c + 1, chunks - 1))
+
+        def tile(r):
+            at = rows(r)
+            g = d32[at, cols(c)]
+            prev = jnp.where(c == 0, hl[0, at, :].astype(jnp.float32), d32[at, prev_at])
+            after = jnp.where(c == chunks - 1, hl[1, at, :].astype(jnp.float32), d32[at, next_at])
+            g_left = jnp.where(lane < NY, pltpu.roll(prev, NY, 1), pltpu.roll(g, NY, 1))
+            g_right = jnp.where(lane >= WIDE - NY, pltpu.roll(after, WIDE - NY, 1),
+                                pltpu.roll(g, WIDE - NY, 1))
+            below = jnp.where(low_wall, 0.0, pltpu.roll(g, 1, 1))
+            above = jnp.where(up_wall, 0.0, pltpu.roll(g, WIDE - 1, 1))
+            moved = (coef[at, 0:1] * (g - g_left) + coef[at, 1:2] * (g_right - g)
+                     + coef[at, 2:3] * (g - below) + coef[at, 3:4] * (above - g))
+            out[at, cols(c)] = g - moved - coef[at, 4:5] * g + dot(ks, r, z, 0, c)
+        loop(PARTS, tile)
+
+    loop(chunks, local)
+
+    def add_mate(c):
+        def tile(r):
+            out[rows(r), cols(c)] += dot(ks, r, mate, 1, c)
+        loop(PARTS, tile)
+
+    @pl.when(jnp.logical_not(mid))
+    def _():
+        def mates(c):
+            to_mate(c).wait_recv()
+            add_mate(c)
+        loop(chunks, mates)
+
+        def others(c):
+            partial(c).wait_recv()
+
+            def tile(r):
+                out[rows(r), cols(c)] += pb[c, rows(r), :].astype(jnp.float32)
+            loop(PARTS, tile)
+        loop(chunks, others)
+        loop(chunks, lambda c: to_mate(c).wait_send())
+
+    @pl.when(mid)
+    def _():
+        def mates(c):
+            to_mate(c).wait_recv()
+            pass_on(c).start()
+            add_mate(c)
+
+        kern_out.wait_recv()
+        over_x[0].start()
+        over_y[0].start()
+        span(0, 2, mates)
+        over_x[1].wait_recv()
+        over_xy[0].start()
+        span(2, 5, mates)
+        over_y[1].wait_recv()
+        over_xy[1].wait_recv()
+        for pair in over_core:
+            pair[0].start()
+        for pair in over_core:
+            pair[1].wait_recv()
+
+        base = (1 - half) * 2
+
+        def finish(c):
+            @pl.when(c + 5 < chunks)
+            def _():
+                mates(c + 5)
+
+            to_peer(c).wait_recv()
+            pass_on(c).wait_recv()
+
+            def flux_tile(r, total):
+                at = rows(r)
+                part = (coef[at, 9:10] * db[2, c, at, :].astype(jnp.float32)
+                        + coef[at, 10:11] * db[3, c, at, :].astype(jnp.float32))
+                return total + jnp.sum(part, axis=0, keepdims=True)
+            flux = lax.fori_loop(0, PARTS, flux_tile, jnp.zeros((1, WIDE), jnp.float32))
+            diffuse = flux * lanes[0:1, cols(c)]
+            specular = lanes[1:2, cols(c)]
+
+            def send_tile(r):
+                at, flipped = rows(r), rows(PARTS - 1 - r)
+                wall = (coef[at, 7:8] * diffuse
+                        + coef[at, 8:9] * specular * db[3, c, flipped, :].astype(jnp.float32))
+                total = wall + dot(ke, r, peer - base, 2, c) + dot(ke, r, far - base, 3, c)
+                pb[c, at, :] = total.astype(jnp.bfloat16)
+            loop(PARTS, send_tile)
+            partial(c).start()
+
+            def own_tile(r):
+                at, flipped = rows(r), rows(PARTS - 1 - r)
+                wall = (coef[at, 5:6] * diffuse
+                        + coef[at, 6:7] * specular * db[2, c, flipped, :].astype(jnp.float32))
+                out[at, cols(c)] += wall + dot(ks, r, peer, 2, c) + dot(ks, r, far, 3, c)
+            loop(PARTS, own_tile)
+
+        loop(chunks, finish)
+        for pair in (over_x, over_y, over_xy, *over_core):
+            pair[0].wait_send()
+
+        def drain(c):
+            to_mate(c).wait_send()
+            to_peer(c).wait_send()
+            pass_on(c).wait_send()
+            partial(c).wait_send()
+        loop(chunks, drain)
+
+    to_right.wait_send()
+    to_left.wait_send()
+
+
+def per_device_line(distribution, kernel, frequency, accommodation, wall_class):
+    vel_rows, cell_count = distribution.shape
+    chunks = cell_count // WIDE
+    z = lax.axis_index("vel")
+    mate = z + 1 - 2 * lax.rem(z, 2)
+    row = lax.iota(jnp.int32, vel_rows)
+    normal_sum, outflow = grid_constants()
+
+    def parts(block):
+        vx, vy, vz = velocity_parts(block * vel_rows + row)
+        speed = jnp.abs(vy)
+        return vx, vy, speed, jnp.exp(-0.5 * (vx * vx + vy * vy + vz * vz)) / normal_sum
+
+    vx, vy, speed, maxwell = parts(z)
+    _, _, mate_speed, mate_maxwell = parts(mate)
+    _, _, peer_speed, _ = parts(3 - z)
+    _, _, far_speed, _ = parts(3 - mate)
+    values = [
+        courant_x * jnp.maximum(vx, 0.0), courant_x * jnp.minimum(vx, 0.0),
+        courant_y * jnp.maximum(vy, 0.0), courant_y * jnp.minimum(vy, 0.0), frequency,
+        courant_y * speed * maxwell / outflow, courant_y * speed,
+        courant_y * mate_speed * mate_maxwell / outflow, courant_y * mate_speed,
+        peer_speed, far_speed,
+    ]
+    place = lax.broadcasted_iota(jnp.int32, (vel_rows, WIDE), 1)
+    coef = jnp.zeros((vel_rows, WIDE), jnp.float32)
+    for i, value in enumerate(values):
+        coef = jnp.where(place == i, value[:, None], coef)
+    low_side = z >= 2
+    classes = jnp.where(low_side, wall_class[0], wall_class[1])
+    ids = lax.iota(jnp.int32, NCLASS)
+    alpha = jnp.sum(jnp.where(classes[:, None] == ids[None, :], accommodation[None, :], 0.0), axis=1)
+    wall_y = jnp.where(low_side, 0, NY - 1)
+    at_wall = lax.iota(jnp.int32, NY) == wall_y
+    both = jnp.stack([alpha, 1.0 - alpha])
+    lanes = jnp.where(at_wall[None, None, :], both[:, :, None], 0.0).reshape(2, cell_count)
+    lanes = jnp.concatenate([lanes, jnp.zeros((6, cell_count), jnp.float32)])
+    dma = pltpu.SemaphoreType.DMA
+    vmem = pl.BlockSpec(memory_space=pltpu.VMEM)
+    any_space = pl.BlockSpec(memory_space=pl.ANY)
+    return pl.pallas_call(
+        gain_kernel,
+        out_shape=jax.ShapeDtypeStruct(distribution.shape, jnp.float32),
+        in_specs=[any_space, any_space, vmem, vmem],
+        out_specs=vmem,
+        scratch_shapes=[
+            pltpu.VMEM((ROWS, cell_count), jnp.float32),
+            pltpu.VMEM((ROWS, PARTS * ROWS), jnp.bfloat16),
+            pltpu.VMEM((ROWS, 2 * ROWS), jnp.bfloat16),
+            pltpu.VMEM((PARTS, chunks, ROWS, WIDE), jnp.bfloat16),
+            pltpu.VMEM((chunks, ROWS, WIDE), jnp.bfloat16),
+            pltpu.VMEM((2, ROWS, WIDE), jnp.bfloat16),
+            dma((2,)),
+            *[dma((chunks,))] * 8,
+            dma((8,)), dma((8,)), dma((2,)), dma((2,)),
+        ],
+        compiler_params=pltpu.CompilerParams(
+            collective_id=0, has_side_effects=True, vmem_limit_bytes=56 << 20),
+        cost_estimate=pl.CostEstimate(flops=12 * ROWS ** 3, bytes_accessed=24 << 20, transcendentals=0),
+    )(distribution, kernel, coef, lanes)
+
+
 def solution(mesh):
+    line = mesh.shape["vel"] == PARTS and mesh.shape["space"] == SPACE
+    body = per_device_line if line else per_device
     placed = (P("vel", "space"), P("vel", None), P("vel"), P(), P(None, "space"))
     return jax.shard_map(
-        per_device, mesh=mesh, in_specs=placed, out_specs=P("vel", "space"), check_vma=False
-    )
+        body, mesh=mesh, in_specs=placed, out_specs=P("vel", "space"), check_vma=False
+    )

time: 197 us -> 128 us (0.65)
  Pallas kernels: 0 us -> 113 us
  waiting for transfers between devices: 86.2 us -> 0 us
  local copies, waits for them, and re-layouts: 41.6 us -> 5.66 us
  matrix products: 21 us -> 0 us
  blocking collectives: 15.5 us -> 0 us
  between operations: 16.3 us -> 3.33 us
  other arithmetic: 11.4 us -> 6.3 us
  starting transfers between devices: 4.71 us -> 0 us
    pallas_call x0 -> x1, Pallas kernels: none -> 113 us  [per_device_line(): pl.pallas_call(gain_kernel, out_shape=jax.ShapeDtypeStruct(distribution.s...]
    all_gather x1 -> x0, waiting for transfers between devices: 79.4 us -> none  [per_device(): shard_piece = lax.all_gather(lowered, 'vel', axis=0, tiled=True)]
    dot_general x1 -> x0, matrix products: 21 us -> none  [per_device(): running = jnp.dot(kernel, shard_piece, preferred_element_type=jnp.float32)]
    slice x5 -> x0, local copies, waits for them, and re-layouts: 20.3 us -> none  [the longest x2 9.83 us: per_device(): walls = jnp.stack([lowered[:, 0::NY], lowered[:, NY - 1::NY]])]
    psum x1 -> x0, blocking collectives: 15.5 us -> none  [per_device(): flux = lax.psum(partial_flux, 'vel')]
    reshape x3 -> x0, local copies, waits for them, and re-layouts: 11 us -> none  [the longest x1 5.52 us: per_device(): jnp.repeat(inflow[0], NY, axis=1)]
    convert_element_type x3 -> x0, other arithmetic: 7.99 us -> none  [the longest x1 4.14 us: per_device(): extended(distribution.astype(jnp.bfloat16), (('space', 1),), NY)]
    ppermute x4 -> x0, waiting for transfers between devices: 6.73 us -> none  [the longest x2 6.73 us: swapped(): lax.ppermute(value, axis, [(i, i ^ 1 << distance) for i in range(lax.axis...]
  transfers between devices with their start and end apart: 5 -> 0, of which waited for: 2 -> 0; matrix products, arithmetic and copies ran while one was open for 25% -> 0% of each run, Pallas kernels for 0% -> 0%
where the time goes in v1:
time: 128 us
  Pallas kernels  113 us (88%)
  other arithmetic  6.3 us (5%)
  local copies, waits for them, and re-layouts  5.66 us (4%)
  between operations  3.33 us (3%)
    pallas_call x1, Pallas kernels, per_device_line(): pl.pallas_call(gain_kernel, out_shape=jax.ShapeDtypeStruct(distribution.s...  113 us
    unnamed x1, local copies, waits for them, and re-layouts  4.79 us
    select_n x1, other arithmetic, per_device_line(): coef = jnp.where(place == i, value[:, None], coef)  3.36 us

profile of v1, /device:TPU:0, one launch (start us, length us, event | category | flops | bytes accessed | tf_op | source)
XLA Modules:
  0.0 128.0 jit_solution(16402445449680781679)
XLA Ops:
  0.0 0.6 fusion.65
  2.5 0.6 fusion.63
  4.5 0.8 fusion.62
  5.3 0.7 select_reduce_fusion
  6.1 0.1 broadcast_in_dim.131
  6.3 0.1 broadcast_in_dim.135
  6.4 0.1 broadcast_in_dim.136
  6.5 0.6 concatenate.3.lanes
  7.1 3.4 %select_select_fusion.coef = f32[1024,128]{1,0:T(8,128)} fusion(f32[1024]{0:T(1024)S(1)} %get-tuple-element.5, f32[1024]{0:T(1024)S(1)} %get-tuple-element.6, f32[1024]{0:T(1024)S(1)} %get-tuple-element.7, f32[1024]{0:T(1024)S(1)} %get-tuple-element.8, f32[1024]{0:T(1024)} %param.7, f32[1024]{0:T(1024)S(1)} %get-tuple-element.10, ...), kind=kLoop, calls=%fused_computation | loop fusion | flops 1441792 | bytes 570752 | tf_op jit(solution)/shard_map/jit(_where)/select_n | solution.py:404
  10.5 112.7 %shard_map.55 = f32[1024,1024]{1,0:T(8,128)} custom-call(f32[1024,1024]{1,0:T(8,128)} %dist.1, bf16[1024,4096]{1,0:T(8,128)(2,1)} %kern.1, f32[1024,128]{1,0:T(8,128)} %select_select_fusion.coef, f32[8,1024]{1,0:T(8,128)} %concatenate.3.lanes), custom_call_target="tpu_custom_call" | custom-call | flops 12884901888 | bytes 25165824 | tf_op jit(solution)/shard_map/pallas_call | solution.py:417
  123.2 4.8 %copy.7 = f32[1024,1024]{1,0:T(8,128)} copy(f32[1024,1024]{1,0:T(8,128)} %shard_map.55) | data formatting | bytes 8388608
  (16 shorter events, 0.2 us)

commit v2 on v1

--- a/solution.py
+++ b/solution.py
@@ -1,3 +1,5 @@
+import math
+
 import jax
 import jax.numpy as jnp
 from jax import lax
@@ -131,9 +133,14 @@
 SPACE = 8
 
 
-def gain_kernel(dist, kern, coef, lanes, out, d32, ks, ke, db, pb, hl,
+def step_kernel(dist, kern, freq, accom, wall_class, out, d32, ks, ke, db, pb, hl, coef, fcol, acc,
                 lsem, s1, r1, s2, r2, s3, r3, s4, r4, sk, rk, sh, rh):
     chunks = dist.shape[1] // WIDE
+    per_chunk = WIDE // NY
+    spacing, middle = 9.6 / NV1, (NV1 - 1) / 2.0
+    points = [(i - middle) * spacing for i in range(NV1)]
+    zsum = sum(math.exp(-0.5 * p * p) for p in points)
+    outflow = sum(p * math.exp(-0.5 * p * p) for p in points if p > 0) / zsum
     sp, z = lax.axis_index("space"), lax.axis_index("vel")
     half = lax.div(z, 2)
     mid = lax.rem(z, 2) + half == 1
@@ -173,11 +180,6 @@
         greet(by_core, z)
         greet(by_x, z)
         greet(by_y, z)
-        pl.semaphore_wait(barrier, 7)
-
-    @pl.when(jnp.logical_not(mid))
-    def _():
-        pl.semaphore_wait(barrier, 3)
 
     def slab(owner):
         return ke.at[pl.ds(pl.multiple_of(owner * (ROWS // SPACE), ROWS // SPACE), ROWS // SPACE)]
@@ -189,7 +191,10 @@
     to_mate = lambda c: remote(db.at[0, c], db.at[1, c], s1.at[c], r1.at[c], sp, mate)
     to_peer = lambda c: remote(db.at[0, c], db.at[2, c], s2.at[c], r2.at[c], sp, peer)
     pass_on = lambda c: remote(db.at[1, c], db.at[3, c], s3.at[c], r3.at[c], sp, peer)
-    partial = lambda c: remote(pb.at[c], pb.at[c], s4.at[c], r4.at[c], sp, mate)
+    def partial(c, r):
+        part = pb.at[c, pl.ds(pl.multiple_of(r * TILE, TILE), TILE)]
+        return remote(part, part, s4.at[c, r], r4.at[c, r], sp, mate)
+
     to_right = remote(db.at[0, chunks - 1], hl.at[0], sh.at[0], rh.at[0], right, z)
     to_left = remote(db.at[0, 0], hl.at[1], sh.at[1], rh.at[1], left, z)
 
@@ -203,10 +208,6 @@
     over_core = [plan(mine, mine + by_core - sp, 4 + i, by_core)
                  for i, mine in enumerate((sp, by_x, by_y, by_xy))]
 
-    @pl.when(jnp.logical_not(mid))
-    def _():
-        kern_out.start()
-
     load_d.wait()
 
     def cols(c):
@@ -232,17 +233,47 @@
             db[0, c, rows(r), :] = d32[rows(r), cols(c)].astype(jnp.bfloat16)
         loop(PARTS, tile)
 
-    def lower_send(c):
-        lower(c)
-
-        @pl.when(mid)
-        def _():
+    loop(chunks, lower)
+
+    @pl.when(mid)
+    def _():
+        pl.semaphore_wait(barrier, 7)
+
+        def send(c):
             to_peer(c).start()
             to_mate(c).start()
-
-    loop(chunks, lower_send)
+        loop(chunks, send)
+
+    @pl.when(jnp.logical_not(mid))
+    def _():
+        pl.semaphore_wait(barrier, 3)
+        kern_out.start()
+
     to_right.start()
     to_left.start()
+
+    plane = lax.broadcasted_iota(jnp.int32, (TILE, WIDE), 0)
+    place = lax.broadcasted_iota(jnp.int32, (TILE, WIDE), 1)
+    vel_x = (lax.div(plane, NV1).astype(jnp.float32) - middle) * spacing
+    vel_z = (lax.rem(plane, NV1).astype(jnp.float32) - middle) * spacing
+    coef[...] = jnp.where(
+        place == 0, courant_x * jnp.maximum(vel_x, 0.0),
+        jnp.where(place == 1, courant_x * jnp.minimum(vel_x, 0.0), vel_x * vel_x + vel_z * vel_z))
+    square = (lax.broadcasted_iota(jnp.int32, (WIDE, WIDE), 0)
+              == lax.broadcasted_iota(jnp.int32, (WIDE, WIDE), 1))
+    for i in range(ROWS // WIDE):
+        fcol[i * WIDE : (i + 1) * WIDE, 0:1] = jnp.sum(
+            jnp.where(square, freq[i : i + 1, :], 0.0), axis=1, keepdims=True)
+
+    def vel_y(block, r):
+        return ((block * PARTS + r).astype(jnp.float32) - middle) * spacing
+
+    def speed(block, r):
+        return jnp.maximum(vel_y(block, r), -vel_y(block, r))
+
+    def maxwell(block, r):
+        vy = vel_y(block, r)
+        return jnp.exp(-0.5 * (coef[:, 2:3] + vy * vy)) * (1.0 / zsum ** 3)
 
     @pl.when(jnp.logical_not(mid))
     def _():
@@ -267,6 +298,7 @@
 
         def tile(r):
             at = rows(r)
+            vy = vel_y(z, r)
             g = d32[at, cols(c)]
             prev = jnp.where(c == 0, hl[0, at, :].astype(jnp.float32), d32[at, prev_at])
             after = jnp.where(c == chunks - 1, hl[1, at, :].astype(jnp.float32), d32[at, next_at])
@@ -275,9 +307,10 @@
                                 pltpu.roll(g, WIDE - NY, 1))
             below = jnp.where(low_wall, 0.0, pltpu.roll(g, 1, 1))
             above = jnp.where(up_wall, 0.0, pltpu.roll(g, WIDE - 1, 1))
-            moved = (coef[at, 0:1] * (g - g_left) + coef[at, 1:2] * (g_right - g)
-                     + coef[at, 2:3] * (g - below) + coef[at, 3:4] * (above - g))
-            out[at, cols(c)] = g - moved - coef[at, 4:5] * g + dot(ks, r, z, 0, c)
+            moved = (coef[:, 0:1] * (g - g_left) + coef[:, 1:2] * (g_right - g)
+                     + courant_y * jnp.maximum(vy, 0.0) * (g - below)
+                     + courant_y * jnp.minimum(vy, 0.0) * (above - g))
+            out[at, cols(c)] = g - moved - fcol[at, 0:1] * g + dot(ks, r, z, 0, c)
         loop(PARTS, tile)
 
     loop(chunks, local)
@@ -295,9 +328,8 @@
         loop(chunks, mates)
 
         def others(c):
-            partial(c).wait_recv()
-
             def tile(r):
+                partial(c, r).wait_recv()
                 out[rows(r), cols(c)] += pb[c, rows(r), :].astype(jnp.float32)
             loop(PARTS, tile)
         loop(chunks, others)
@@ -332,31 +364,46 @@
                 mates(c + 5)
 
             to_peer(c).wait_recv()
+
+            def near_tile(r, total):
+                at = rows(r)
+                acc[at, :] = dot(ke, r, peer - base, 2, c)
+                out[at, cols(c)] += dot(ks, r, peer, 2, c)
+                part = speed(peer, r) * db[2, c, at, :].astype(jnp.float32)
+                return total + jnp.sum(part, axis=0, keepdims=True)
+            flux = lax.fori_loop(0, PARTS, near_tile, jnp.zeros((1, WIDE), jnp.float32))
+
             pass_on(c).wait_recv()
 
             def flux_tile(r, total):
+                part = speed(far, r) * db[3, c, rows(r), :].astype(jnp.float32)
+                return total + jnp.sum(part, axis=0, keepdims=True)
+            flux = lax.fori_loop(0, PARTS, flux_tile, flux)
+
+            spot = lax.broadcasted_iota(jnp.int32, (1, WIDE), 1)
+            alpha = jnp.zeros((1, WIDE), jnp.float32)
+            specular = alpha
+            for j in range(per_chunk):
+                value = accom[wall_class[1 - half, c * per_chunk + j]]
+                here = spot == j * NY + (1 - half) * (NY - 1)
+                alpha = jnp.where(here, value, alpha)
+                specular = jnp.where(here, 1.0 - value, specular)
+            diffuse = flux * alpha * (1.0 / outflow)
+
+            def wall(block, r, slot):
+                mirror = db[slot, c, rows(PARTS - 1 - r), :].astype(jnp.float32)
+                return courant_y * speed(block, r) * (diffuse * maxwell(block, r) + specular * mirror)
+
+            def send_tile(r):
                 at = rows(r)
-                part = (coef[at, 9:10] * db[2, c, at, :].astype(jnp.float32)
-                        + coef[at, 10:11] * db[3, c, at, :].astype(jnp.float32))
-                return total + jnp.sum(part, axis=0, keepdims=True)
-            flux = lax.fori_loop(0, PARTS, flux_tile, jnp.zeros((1, WIDE), jnp.float32))
-            diffuse = flux * lanes[0:1, cols(c)]
-            specular = lanes[1:2, cols(c)]
-
-            def send_tile(r):
-                at, flipped = rows(r), rows(PARTS - 1 - r)
-                wall = (coef[at, 7:8] * diffuse
-                        + coef[at, 8:9] * specular * db[3, c, flipped, :].astype(jnp.float32))
-                total = wall + dot(ke, r, peer - base, 2, c) + dot(ke, r, far - base, 3, c)
+                total = acc[at, :] + wall(mate, r, 3) + dot(ke, r, far - base, 3, c)
                 pb[c, at, :] = total.astype(jnp.bfloat16)
+                partial(c, r).start()
             loop(PARTS, send_tile)
-            partial(c).start()
 
             def own_tile(r):
-                at, flipped = rows(r), rows(PARTS - 1 - r)
-                wall = (coef[at, 5:6] * diffuse
-                        + coef[at, 6:7] * specular * db[2, c, flipped, :].astype(jnp.float32))
-                out[at, cols(c)] += wall + dot(ks, r, peer, 2, c) + dot(ks, r, far, 3, c)
+                at = rows(r)
+                out[at, cols(c)] += wall(z, r, 2) + dot(ks, r, far, 3, c)
             loop(PARTS, own_tile)
 
         loop(chunks, finish)
@@ -367,7 +414,7 @@
             to_mate(c).wait_send()
             to_peer(c).wait_send()
             pass_on(c).wait_send()
-            partial(c).wait_send()
+            loop(PARTS, lambda r: partial(c, r).wait_send())
         loop(chunks, drain)
 
     to_right.wait_send()
@@ -375,49 +422,16 @@
 
 
 def per_device_line(distribution, kernel, frequency, accommodation, wall_class):
-    vel_rows, cell_count = distribution.shape
+    cell_count = distribution.shape[1]
     chunks = cell_count // WIDE
-    z = lax.axis_index("vel")
-    mate = z + 1 - 2 * lax.rem(z, 2)
-    row = lax.iota(jnp.int32, vel_rows)
-    normal_sum, outflow = grid_constants()
-
-    def parts(block):
-        vx, vy, vz = velocity_parts(block * vel_rows + row)
-        speed = jnp.abs(vy)
-        return vx, vy, speed, jnp.exp(-0.5 * (vx * vx + vy * vy + vz * vz)) / normal_sum
-
-    vx, vy, speed, maxwell = parts(z)
-    _, _, mate_speed, mate_maxwell = parts(mate)
-    _, _, peer_speed, _ = parts(3 - z)
-    _, _, far_speed, _ = parts(3 - mate)
-    values = [
-        courant_x * jnp.maximum(vx, 0.0), courant_x * jnp.minimum(vx, 0.0),
-        courant_y * jnp.maximum(vy, 0.0), courant_y * jnp.minimum(vy, 0.0), frequency,
-        courant_y * speed * maxwell / outflow, courant_y * speed,
-        courant_y * mate_speed * mate_maxwell / outflow, courant_y * mate_speed,
-        peer_speed, far_speed,
-    ]
-    place = lax.broadcasted_iota(jnp.int32, (vel_rows, WIDE), 1)
-    coef = jnp.zeros((vel_rows, WIDE), jnp.float32)
-    for i, value in enumerate(values):
-        coef = jnp.where(place == i, value[:, None], coef)
-    low_side = z >= 2
-    classes = jnp.where(low_side, wall_class[0], wall_class[1])
-    ids = lax.iota(jnp.int32, NCLASS)
-    alpha = jnp.sum(jnp.where(classes[:, None] == ids[None, :], accommodation[None, :], 0.0), axis=1)
-    wall_y = jnp.where(low_side, 0, NY - 1)
-    at_wall = lax.iota(jnp.int32, NY) == wall_y
-    both = jnp.stack([alpha, 1.0 - alpha])
-    lanes = jnp.where(at_wall[None, None, :], both[:, :, None], 0.0).reshape(2, cell_count)
-    lanes = jnp.concatenate([lanes, jnp.zeros((6, cell_count), jnp.float32)])
     dma = pltpu.SemaphoreType.DMA
     vmem = pl.BlockSpec(memory_space=pltpu.VMEM)
+    smem = pl.BlockSpec(memory_space=pltpu.SMEM)
     any_space = pl.BlockSpec(memory_space=pl.ANY)
     return pl.pallas_call(
-        gain_kernel,
-        out_shape=jax.ShapeDtypeStruct(distribution.shape, jnp.float32),
-        in_specs=[any_space, any_space, vmem, vmem],
+        step_kernel,
+        out_shape=pltpu.VMEM(distribution.shape, jnp.float32),
+        in_specs=[any_space, any_space, vmem, smem, smem],
         out_specs=vmem,
         scratch_shapes=[
             pltpu.VMEM((ROWS, cell_count), jnp.float32),
@@ -426,14 +440,17 @@
             pltpu.VMEM((PARTS, chunks, ROWS, WIDE), jnp.bfloat16),
             pltpu.VMEM((chunks, ROWS, WIDE), jnp.bfloat16),
             pltpu.VMEM((2, ROWS, WIDE), jnp.bfloat16),
+            pltpu.VMEM((TILE, WIDE), jnp.float32),
+            pltpu.VMEM((ROWS, WIDE), jnp.float32),
+            pltpu.VMEM((ROWS, WIDE), jnp.float32),
             dma((2,)),
-            *[dma((chunks,))] * 8,
+            *[dma((chunks,))] * 6, dma((chunks, PARTS)), dma((chunks, PARTS)),
             dma((8,)), dma((8,)), dma((2,)), dma((2,)),
         ],
         compiler_params=pltpu.CompilerParams(
             collective_id=0, has_side_effects=True, vmem_limit_bytes=56 << 20),
         cost_estimate=pl.CostEstimate(flops=12 * ROWS ** 3, bytes_accessed=24 << 20, transcendentals=0),
-    )(distribution, kernel, coef, lanes)
+    )(distribution, kernel, frequency.reshape(ROWS // WIDE, WIDE), accommodation, wall_class)
 
 
 def solution(mesh):

time: 128 us -> 111 us (0.87)
  other arithmetic: 6.3 us -> 0 us
  Pallas kernels: 113 us -> 109 us
  local copies, waits for them, and re-layouts: 5.66 us -> 2.02 us
  between operations: 3.33 us -> 0.01 us
    select_n x3 -> x0, other arithmetic: 4.13 us -> none  [the longest x1 3.36 us: per_device_line(): coef = jnp.where(place == i, value[:, None], coef)]
    pallas_call x1, Pallas kernels: 113 us -> 109 us  [per_device_line(): pl.pallas_call(step_kernel, out_shape=pltpu.VMEM(distribution.shape, jnp....]
    unnamed x1, local copies, waits for them, and re-layouts: 4.79 us -> 2.02 us
    reduce_sum x3 -> x0, other arithmetic: 1.99 us -> none  [the longest x1 0.74 us: per_device_line(): jnp.sum(jnp.where(classes[:, None] == ids[None, :], accommodation[None, :...]
where the time goes in v2:
time: 111 us
  Pallas kernels  109 us (98%)
  local copies, waits for them, and re-layouts  2.02 us (2%)
    pallas_call x1, Pallas kernels, per_device_line(): pl.pallas_call(step_kernel, out_shape=pltpu.VMEM(distribution.shape, jnp....  109 us

profile of v2, /device:TPU:0, one launch (start us, length us, event | category | flops | bytes accessed | tf_op | source)
XLA Modules:
  0.0 110.7 jit_solution(9694920882403163029)
XLA Ops:
  0.0 108.6 %shard_map.55 = f32[1024,1024]{1,0:T(8,128)S(1)} custom-call(f32[1024,1024]{1,0:T(8,128)} %dist.1, bf16[1024,4096]{1,0:T(8,128)(2,1)} %kern.1, f32[8,128]{1,0:T(8,128)} %bitcast.1, f32[8]{0:T(128)} %accom.1, s32[2,32]{1,0:T(2,128)} %wall_class.1), custom_call_target="tpu_custom_call" | custom-call | flops 12884901888 | bytes 25165824 | tf_op jit(solution)/shard_map/pallas_call | solution.py:431
  108.7 2.0 %copy.7 = f32[1024,1024]{1,0:T(8,128)} copy(f32[1024,1024]{1,0:T(8,128)S(1)} %shard_map.55) | data formatting | bytes 8388608

commit v3 on v2

--- a/solution.py
+++ b/solution.py
@@ -134,7 +134,7 @@
 
 
 def step_kernel(dist, kern, freq, accom, wall_class, out, d32, ks, ke, db, pb, hl, coef, fcol, acc,
-                lsem, s1, r1, s2, r2, s3, r3, s4, r4, sk, rk, sh, rh):
+                lsem, s1, r1, s2, r2, s3, r3, s4, r4, s5, r5, s6, r6, sk, rk, sh, rh):
     chunks = dist.shape[1] // WIDE
     per_chunk = WIDE // NY
     spacing, middle = 9.6 / NV1, (NV1 - 1) / 2.0
@@ -191,6 +191,17 @@
     to_mate = lambda c: remote(db.at[0, c], db.at[1, c], s1.at[c], r1.at[c], sp, mate)
     to_peer = lambda c: remote(db.at[0, c], db.at[2, c], s2.at[c], r2.at[c], sp, peer)
     pass_on = lambda c: remote(db.at[1, c], db.at[3, c], s3.at[c], r3.at[c], sp, peer)
+    last = chunks - 1
+
+    def tail(slot, r, dst_slot, send, recv, vel):
+        part = pl.ds(pl.multiple_of(r * TILE, TILE), TILE)
+        return remote(db.at[slot, last, part], db.at[dst_slot, last, part],
+                      send.at[r], recv.at[r], sp, vel)
+
+    pass_last = lambda r: tail(1, r, 3, s5, r5, peer)
+    raw_far = lambda r: tail(3, r, 3, s6, r6, mate)
+    raw_near = remote(db.at[2, last], db.at[2, last], s6.at[PARTS], r6.at[PARTS], sp, mate)
+
     def partial(c, r):
         part = pb.at[c, pl.ds(pl.multiple_of(r * TILE, TILE), TILE)]
         return remote(part, part, s4.at[c, r], r4.at[c, r], sp, mate)
@@ -198,14 +209,19 @@
     to_right = remote(db.at[0, chunks - 1], hl.at[0], sh.at[0], rh.at[0], right, z)
     to_left = remote(db.at[0, 0], hl.at[1], sh.at[1], rh.at[1], left, z)
 
-    def plan(out_slab, in_slab, at, target):
-        return (remote(slab(out_slab), slab(out_slab), sk.at[at], rk.at[at], target, z),
-                remote(slab(in_slab), slab(in_slab), sk.at[at], rk.at[at], target, z))
-
-    over_x = plan(sp, by_x, 1, by_x)
-    over_y = plan(sp, by_y, 2, by_y)
-    over_xy = plan(by_x, by_xy, 3, by_y)
-    over_core = [plan(mine, mine + by_core - sp, 4 + i, by_core)
+    def piece(owner, side):
+        part = ROWS // SPACE // 2
+        return ke.at[pl.ds(pl.multiple_of(owner * 2 * part + side * part, part), part)]
+
+    def plan(sent, received, at, target):
+        return (remote(sent, sent, sk.at[at], rk.at[at], target, z),
+                remote(received, received, sk.at[at], rk.at[at], target, z))
+
+    over_x = plan(slab(sp), slab(by_x), 1, by_x)
+    over_y = plan(slab(sp), slab(by_y), 2, by_y)
+    on_y = plan(piece(by_x, 0), piece(by_xy, 0), 3, by_y)
+    on_x = plan(piece(by_y, 1), piece(by_xy, 1), 8, by_x)
+    over_core = [plan(slab(mine), slab(mine + by_core - sp), 4 + i, by_core)
                  for i, mine in enumerate((sp, by_x, by_y, by_xy))]
 
     load_d.wait()
@@ -320,6 +336,46 @@
             out[rows(r), cols(c)] += dot(ks, r, mate, 1, c)
         loop(PARTS, tile)
 
+    def flux_of(block, slot, c, start):
+        def tile(r, total):
+            part = speed(block, r) * db[slot, c, rows(r), :].astype(jnp.float32)
+            return total + jnp.sum(part, axis=0, keepdims=True)
+        return lax.fori_loop(0, PARTS, tile, start)
+
+    def wall_rates(c, flux):
+        spot = lax.broadcasted_iota(jnp.int32, (1, WIDE), 1)
+        alpha = jnp.zeros((1, WIDE), jnp.float32)
+        specular = alpha
+        for j in range(per_chunk):
+            value = accom[wall_class[1 - half, c * per_chunk + j]]
+            here = spot == j * NY + (1 - half) * (NY - 1)
+            alpha = jnp.where(here, value, alpha)
+            specular = jnp.where(here, 1.0 - value, specular)
+        return flux * alpha * (1.0 / outflow), specular
+
+    def wall(rates, block, r, slot, c):
+        diffuse, specular = rates
+        mirror = db[slot, c, rows(PARTS - 1 - r), :].astype(jnp.float32)
+        return courant_y * speed(block, r) * (diffuse * maxwell(block, r) + specular * mirror)
+
+    near = jnp.where(mid, peer, far)
+    rest = jnp.where(mid, far, peer)
+    zero_flux = jnp.zeros((1, WIDE), jnp.float32)
+
+    def close_near():
+        def tile(r):
+            out[rows(r), cols(last)] += dot(ks, r, near, 2, last)
+        loop(PARTS, tile)
+        return flux_of(near, 2, last, zero_flux)
+
+    def close_rest(flux, mirror_slot):
+        rates = wall_rates(last, flux_of(rest, 3, last, flux))
+
+        def tile(r):
+            out[rows(r), cols(last)] += (wall(rates, z, r, mirror_slot, last)
+                                         + dot(ks, r, rest, 3, last))
+        loop(PARTS, tile)
+
     @pl.when(jnp.logical_not(mid))
     def _():
         def mates(c):
@@ -332,14 +388,26 @@
                 partial(c, r).wait_recv()
                 out[rows(r), cols(c)] += pb[c, rows(r), :].astype(jnp.float32)
             loop(PARTS, tile)
-        loop(chunks, others)
+        loop(last, others)
+        raw_near.wait_recv()
+        flux = close_near()
+        loop(PARTS, lambda r: raw_far(r).wait_recv())
+        close_rest(flux, 3)
         loop(chunks, lambda c: to_mate(c).wait_send())
 
     @pl.when(mid)
     def _():
         def mates(c):
             to_mate(c).wait_recv()
-            pass_on(c).start()
+
+            @pl.when(c < last)
+            def _():
+                pass_on(c).start()
+
+            @pl.when(c == last)
+            def _():
+                loop(PARTS, lambda r: pass_last(r).start())
+
             add_mate(c)
 
         kern_out.wait_recv()
@@ -347,10 +415,12 @@
         over_y[0].start()
         span(0, 2, mates)
         over_x[1].wait_recv()
-        over_xy[0].start()
-        span(2, 5, mates)
+        on_y[0].start()
         over_y[1].wait_recv()
-        over_xy[1].wait_recv()
+        on_x[0].start()
+        span(2, 4, mates)
+        on_y[1].wait_recv()
+        on_x[1].wait_recv()
         for pair in over_core:
             pair[0].start()
         for pair in over_core:
@@ -359,10 +429,6 @@
         base = (1 - half) * 2
 
         def finish(c):
-            @pl.when(c + 5 < chunks)
-            def _():
-                mates(c + 5)
-
             to_peer(c).wait_recv()
 
             def near_tile(r, total):
@@ -375,47 +441,55 @@
 
             pass_on(c).wait_recv()
 
-            def flux_tile(r, total):
-                part = speed(far, r) * db[3, c, rows(r), :].astype(jnp.float32)
-                return total + jnp.sum(part, axis=0, keepdims=True)
-            flux = lax.fori_loop(0, PARTS, flux_tile, flux)
-
-            spot = lax.broadcasted_iota(jnp.int32, (1, WIDE), 1)
-            alpha = jnp.zeros((1, WIDE), jnp.float32)
-            specular = alpha
-            for j in range(per_chunk):
-                value = accom[wall_class[1 - half, c * per_chunk + j]]
-                here = spot == j * NY + (1 - half) * (NY - 1)
-                alpha = jnp.where(here, value, alpha)
-                specular = jnp.where(here, 1.0 - value, specular)
-            diffuse = flux * alpha * (1.0 / outflow)
-
-            def wall(block, r, slot):
-                mirror = db[slot, c, rows(PARTS - 1 - r), :].astype(jnp.float32)
-                return courant_y * speed(block, r) * (diffuse * maxwell(block, r) + specular * mirror)
+            rates = wall_rates(c, flux_of(far, 3, c, flux))
 
             def send_tile(r):
                 at = rows(r)
-                total = acc[at, :] + wall(mate, r, 3) + dot(ke, r, far - base, 3, c)
+                total = acc[at, :] + wall(rates, mate, r, 3, c) + dot(ke, r, far - base, 3, c)
                 pb[c, at, :] = total.astype(jnp.bfloat16)
                 partial(c, r).start()
             loop(PARTS, send_tile)
 
+            @pl.when(c + 4 < chunks)
+            def _():
+                mates(c + 4)
+
+            @pl.when(c == 3)
+            def _():
+                to_peer(last).wait_recv()
+                raw_near.start()
+
             def own_tile(r):
                 at = rows(r)
-                out[at, cols(c)] += wall(z, r, 2) + dot(ks, r, far, 3, c)
+                out[at, cols(c)] += wall(rates, z, r, 2, c) + dot(ks, r, far, 3, c)
             loop(PARTS, own_tile)
 
-        loop(chunks, finish)
-        for pair in (over_x, over_y, over_xy, *over_core):
+        loop(last, finish)
+        flux = close_near()
+
+        def relay(r):
+            pass_last(r).wait_recv()
+            raw_far(r).start()
+        loop(PARTS, relay)
+        close_rest(flux, 2)
+        for pair in (over_x, over_y, on_x, on_y, *over_core):
             pair[0].wait_send()
 
         def drain(c):
             to_mate(c).wait_send()
             to_peer(c).wait_send()
-            pass_on(c).wait_send()
-            loop(PARTS, lambda r: partial(c, r).wait_send())
+
+            @pl.when(c < last)
+            def _():
+                pass_on(c).wait_send()
+                loop(PARTS, lambda r: partial(c, r).wait_send())
         loop(chunks, drain)
+        raw_near.wait_send()
+
+        def drain_last(r):
+            pass_last(r).wait_send()
+            raw_far(r).wait_send()
+        loop(PARTS, drain_last)
 
     to_right.wait_send()
     to_left.wait_send()
@@ -445,7 +519,8 @@
             pltpu.VMEM((ROWS, WIDE), jnp.float32),
             dma((2,)),
             *[dma((chunks,))] * 6, dma((chunks, PARTS)), dma((chunks, PARTS)),
-            dma((8,)), dma((8,)), dma((2,)), dma((2,)),
+            dma((PARTS,)), dma((PARTS,)), dma((PARTS + 1,)), dma((PARTS + 1,)),
+            dma((9,)), dma((9,)), dma((2,)), dma((2,)),
         ],
         compiler_params=pltpu.CompilerParams(
             collective_id=0, has_side_effects=True, vmem_limit_bytes=56 << 20),

time: 111 us -> 116 us (1.045)
  Pallas kernels: 109 us -> 114 us
    pallas_call x1, Pallas kernels: 109 us -> 114 us  [per_device_line(): pl.pallas_call(step_kernel, out_shape=pltpu.VMEM(distribution.shape, jnp....]
where the time goes in v3:
time: 116 us
  Pallas kernels  114 us (98%)
  local copies, waits for them, and re-layouts  2.02 us (2%)
    pallas_call x1, Pallas kernels, per_device_line(): pl.pallas_call(step_kernel, out_shape=pltpu.VMEM(distribution.shape, jnp....  114 us

profile of v3, /device:TPU:0, one launch (start us, length us, event | category | flops | bytes accessed | tf_op | source)
XLA Modules:
  0.0 115.6 jit_solution(18116312336212822907)
XLA Ops:
  0.0 113.5 %shard_map.55 = f32[1024,1024]{1,0:T(8,128)S(1)} custom-call(f32[1024,1024]{1,0:T(8,128)} %dist.1, bf16[1024,4096]{1,0:T(8,128)(2,1)} %kern.1, f32[8,128]{1,0:T(8,128)} %bitcast.1, f32[8]{0:T(128)} %accom.1, s32[2,32]{1,0:T(2,128)} %wall_class.1), custom_call_target="tpu_custom_call" | custom-call | flops 12884901888 | bytes 25165824 | tf_op jit(solution)/shard_map/pallas_call | solution.py:505
  113.5 2.0 %copy.7 = f32[1024,1024]{1,0:T(8,128)} copy(f32[1024,1024]{1,0:T(8,128)S(1)} %shard_map.55) | data formatting | bytes 8388608
